TPU v7x, 128 devices: a whole 4x4x4 slice. The times are simulated.
128 devices in a mesh: fly: 16 (over y, z), sub: 8 (over x, core).
Axes of the slice: x: 4, y: 4, z: 4, core: 2. Of those that a mesh axis runs over, the one named last changes fastest.
Arguments:
- matrix: float32 [16384, 2048], P(('fly', 'sub'))
- row_signs: int32 [16384], P(('fly', 'sub')), may hold values from -1 to 1, as said below
- sample_idx: int32 [4096], P(('fly', 'sub')), may hold values from 0 to 127, as said below
- ridge_shift: float32 [1], replicated, may hold values from 0.5 to 1.5
Outputs:
- chol: float32 [2048, 2048], P(('fly', 'sub'))
- col_norms: float32 [2048], replicated
Inputs may be any that keep to these rules, and one draw needn't show every extreme that they name: `sample_idx`: within each aligned block of 32 entries the row numbers are distinct. `row_signs`: each entry is -1 or 1.
All inputs are finite; a program needn't handle non-finite values.
Results may differ from a plain program's by a relative error of at most 0.00022.
Values sent between devices are 32-bit elements; how exact they have to be, the bound alone decides.
No kernel may reach another device: no remote copies, remote signals or barrier semaphores. Data moves between devices by JAX's collectives and lax.ppermute only.
A program may use at most 192 MiB of HBM per device.

v0:
```python
import math

import jax
import jax.numpy as jnp
from jax import lax
from jax.sharding import PartitionSpec as P


def swapped(value, axis, stride):
    mask = 2**stride
    pairs = [(source, source ^ mask) for source in range(lax.axis_size(axis))]
    return lax.ppermute(value, axis, pairs)


def sylvester(order):
    digits = order.bit_length() - 1
    indices = jnp.arange(order, dtype=jnp.int32)
    common_bits = indices[:, None] & indices[None, :]
    parity = jnp.zeros((order, order), jnp.int32)
    for bit_pos in range(digits):
        parity = parity ^ common_bits >> bit_pos & 1
    return (1 - 2 * parity).astype(jnp.float32)


def shards(matrix, row_signs, sample_idx, ridge_shift):
    rows_here, columns = matrix.shape
    devices_all = lax.axis_size(("fly", "sub"))
    total_rows = rows_here * devices_all
    sign_column = row_signs.astype(jnp.float32)[:, None]
    col_squares = lax.psum(jnp.sum(matrix * matrix, axis=0), ("fly", "sub"))
    col_norms = jnp.sqrt(col_squares / total_rows + 1e-06)
    signed = matrix * sign_column / col_norms[None, :]
    local_table = sylvester(rows_here)
    transformed = jnp.dot(
        local_table, signed, precision=lax.Precision.HIGHEST, preferred_element_type=jnp.float32
    )
    for bit_pos in range(lax.axis_size("fly").bit_length() - 1):
        partner = swapped(transformed, "fly", bit_pos)
        is_low = lax.axis_index("fly") >> bit_pos & 1 == 0
        transformed = jnp.where(is_low, transformed + partner, partner - transformed)
    for bit_pos in range(lax.axis_size("sub").bit_length() - 1):
        partner = swapped(transformed, "sub", bit_pos)
        is_low = lax.axis_index("sub") >> bit_pos & 1 == 0
        transformed = jnp.where(is_low, transformed + partner, partner - transformed)
    picked = jnp.take(transformed, sample_idx, axis=0) / math.sqrt(total_rows)
    samples_all = picked.shape[0] * devices_all
    gram_share = lax.psum_scatter(
        jnp.dot(
            picked.T, picked, precision=lax.Precision.HIGHEST, preferred_element_type=jnp.float32
        ),
        ("fly", "sub"),
        scatter_dimension=0,
        tiled=True,
    )
    gram_full = lax.all_gather(gram_share, ("fly", "sub"), axis=0, tiled=True)
    gram_full = gram_full / samples_all + ridge_shift[0] * jnp.eye(columns, dtype=jnp.float32)
    factor = jnp.linalg.cholesky(gram_full)
    share_rows = columns // devices_all
    chol = lax.dynamic_slice_in_dim(
        factor, lax.axis_index(("fly", "sub")) * share_rows, share_rows, 0
    )
    return (chol, col_norms)


def solution(mesh):
    in_specs = (P(("fly", "sub"), None), P(("fly", "sub")), P(("fly", "sub")), P())
    out_specs = (P(("fly", "sub"), None), P())
    return jax.shard_map(shards, mesh=mesh, in_specs=in_specs, out_specs=out_specs, check_vma=False)
```

profile of v0, /device:TPU:1, one launch (start us, length us, event | category | flops | bytes accessed | tf_op | source)
XLA Modules:
  0.0 1567.8 jit_solution(2420126985644542747)
XLA Ops:
  8.5 68.7 %psum.7 = f32[2048]{0:T(1024)S(1)} all-reduce(f32[2048]{0:T(1024)S(1)} %multiply_reduce_fusion), channel_id=1, replica_groups=mesh['fly'=16,'sub'=8] {'fly','sub'}, use_global_device_ids=true, to_apply=%region_1.0 | all-reduce | flops 2048 | bytes 16384 | tf_op jit(solution)/shard_map/psum | solution.py:30
  80.4 23.7 %collective-permute-done = f32[128,2048]{1,0:T(8,128)S(1)} collective-permute-done((f32[128,2048]{1,0:T(8,128)S(1)}, f32[128,2048]{1,0:T(8,128)S(1)}, u32[]{:S(2)}, u32[]{:S(2)}) %collective-permute-start) | collective-permute-done | bytes 1048608 | tf_op jit(solution)/shard_map/ppermute | solution.py:12
  105.5 23.1 %collective-permute-done.1 = f32[128,2048]{1,0:T(8,128)S(1)} collective-permute-done((f32[128,2048]{1,0:T(8,128)S(1)}, f32[128,2048]{1,0:T(8,128)S(1)}, u32[]{:S(2)}, u32[]{:S(2)}) %collective-permute-start.1) | collective-permute-done | bytes 1048608 | tf_op jit(solution)/shard_map/ppermute | solution.py:12
  128.9 21.9 %collective-permute-done.2 = f32[128,2048]{1,0:T(8,128)S(1)} collective-permute-done((f32[128,2048]{1,0:T(8,128)S(1)}, f32[128,2048]{1,0:T(8,128)S(1)}, u32[]{:S(2)}, u32[]{:S(2)}) %collective-permute-start.2) | collective-permute-done | bytes 1048608 | tf_op jit(solution)/shard_map/ppermute | solution.py:12
  152.5 21.1 %collective-permute-done.3 = f32[128,2048]{1,0:T(8,128)S(1)} collective-permute-done((f32[128,2048]{1,0:T(8,128)S(1)}, f32[128,2048]{1,0:T(8,128)S(1)}, u32[]{:S(2)}, u32[]{:S(2)}) %collective-permute-start.3) | collective-permute-done | bytes 1048608 | tf_op jit(solution)/shard_map/ppermute | solution.py:12
  181.8 23.5 %collective-permute-done.5 = f32[128,2048]{1,0:T(8,128)S(1)} collective-permute-done((f32[128,2048]{1,0:T(8,128)S(1)}, f32[128,2048]{1,0:T(8,128)S(1)}, u32[]{:S(2)}, u32[]{:S(2)}) %collective-permute-start.5) | collective-permute-done | bytes 1048608 | tf_op jit(solution)/shard_map/ppermute | solution.py:12
  207.5 23.0 %collective-permute-done.6 = f32[128,2048]{1,0:T(8,128)S(1)} collective-permute-done((f32[128,2048]{1,0:T(8,128)S(1)}, f32[128,2048]{1,0:T(8,128)S(1)}, u32[]{:S(2)}, u32[]{:S(2)}) %collective-permute-start.6) | collective-permute-done | bytes 1048608 | tf_op jit(solution)/shard_map/ppermute | solution.py:12
  231.3 16.2 %fusion.93 = f32[2048,2048]{1,0:T(8,128)} fusion(f32[32,2048]{1,0:T(8,128)S(1)} %gather_fusion, pred[32]{0:T(512)(128)(4,1)S(1)} %compare_and_fusion), kind=kOutput, calls=%fused_computation.100 | convolution fusion | flops 1610743808 | bytes 17039392
  247.5 659.3 %reduce-scatter.4.cloned.1.call-done = f32[16,2048]{1,0:T(8,128)} async-done(((f32[2048,2048]{1,0:T(8,128)}), f32[16,2048]{1,0:T(8,128)}) %reduce-scatter.4.cloned.1.call-update) | async-done | bytes 131088 | tf_op jit(solution)/shard_map/reduce_scatter | solution.py:47
  907.4 83.8 %all-gather.2.cloned.1.call-done = f32[2048,2048]{1,0:T(8,128)} async-done(((f32[16,2048]{1,0:T(8,128)}), f32[2048,2048]{1,0:T(8,128)}) %all-gather.2.cloned.1.call-update) | async-done | bytes 16777232 | tf_op jit(solution)/shard_map/all_gather | solution.py:55
  991.3 17.6 %copy.42 = f32[2048,2048]{0,1:T(8,128)} copy(f32[2048,2048]{1,0:T(8,128)} %all-gather.2.cloned.1.call-done) | data formatting | bytes 33554432 | tf_op jit(solution)/shard_map/all_gather | solution.py:55
  1008.9 12.4 select_add_fusion
  1021.3 17.6 %copy.43 = f32[2048,2048]{1,0:T(8,128)} copy(f32[2048,2048]{0,1:T(8,128)} %select_add_fusion) | data formatting | bytes 33554432 | tf_op jit(solution)/shard_map/add | solution.py:56
  1038.9 12.1 fusion
  1056.7 11.7 cholesky.456
  1068.6 9.8 custom-call.123
  1083.0 11.7 cholesky.479
  1094.8 10.0 custom-call.124
  1118.2 11.7 cholesky.502
  1130.7 10.2 custom-call.125
  1149.0 11.7 cholesky.523
  1161.5 10.0 custom-call.126
  1180.5 11.7 cholesky.960
  1193.0 10.0 custom-call.127
  1212.8 11.7 cholesky.980
  1225.3 10.2 custom-call.128
  1245.8 11.7 cholesky.1000
  1258.3 10.0 custom-call.129
  1269.9 9.1 fusion.23
  1279.0 11.9 cholesky.1020
  1291.7 9.8 custom-call.130
  1302.9 9.1 fusion.41
  1312.1 12.1 cholesky.1040
  1325.0 9.8 custom-call.131
  1336.2 9.1 fusion.44
  1345.3 11.9 cholesky.1060
  1357.9 9.8 custom-call.132
  1377.7 11.9 cholesky.1080
  1390.4 9.8 custom-call.133
  1409.6 12.1 cholesky.1100
  1422.4 9.8 custom-call.134
  1440.6 11.9 cholesky.1120
  1453.3 9.8 custom-call.135
  1470.4 11.9 cholesky.1140
  1483.1 9.8 custom-call.136
  1498.7 11.7 cholesky.1160
  1511.2 9.8 custom-call.137
  1525.5 11.7 cholesky.1178
  (144 shorter events, 153.2 us)
Async XLA Ops:
  7.2 200.3 %copy-start.3 = (s32[32]{0:T(128)S(1)}, s32[32]{0:T(128)}, u32[]{:S(2)}) copy-start(s32[32]{0:T(128)} %param.6) | copy-start | bytes 388
  7.2 899.6 %reduce-scatter.4.cloned.1.call-start = ((), (), s32[]{:S(2)}) async-start(), calls=%async_computation.2 | async-start | bytes 16908288 | tf_op jit(solution)/shard_map/reduce_scatter | solution.py:47
  77.3 170.1 %copy-start.2 = (f32[2048]{0:T(1024)}, f32[2048]{0:T(1024)S(1)}, u32[]{:S(2)}) copy-start(f32[2048]{0:T(1024)S(1)} %add_sqrt_fusion) | copy-start | bytes 24580
  80.3 23.8 %collective-permute-start = (f32[128,2048]{1,0:T(8,128)S(1)}, f32[128,2048]{1,0:T(8,128)S(1)}, u32[]{:S(2)}, u32[]{:S(2)}) collective-permute-start(f32[128,2048]{1,0:T(8,128)S(1)} %fusion.63), channel_id=1, source_target_pairs={{0,8},{8,0},{16,24},{24,16},{32,40},{40,32},{48,56},{56,48},{64,72... | collective-permute-start | bytes 3145736 | tf_op jit(solution)/shard_map/ppermute | solution.py:12
  104.3 24.4 %collective-permute-start.1 = (f32[128,2048]{1,0:T(8,128)S(1)}, f32[128,2048]{1,0:T(8,128)S(1)}, u32[]{:S(2)}, u32[]{:S(2)}) collective-permute-start(f32[128,2048]{1,0:T(8,128)S(1)} %subtract_select_fusion.6), channel_id=1, source_target_pairs={{0,16},{8,24},{16,0},{24,8},{32,48},{40,56},{48,32},{56,40},{64,80... | collective-permute-start | bytes 3145736 | tf_op jit(solution)/shard_map/ppermute | solution.py:12
  128.8 22.0 %collective-permute-start.2 = (f32[128,2048]{1,0:T(8,128)S(1)}, f32[128,2048]{1,0:T(8,128)S(1)}, u32[]{:S(2)}, u32[]{:S(2)}) collective-permute-start(f32[128,2048]{1,0:T(8,128)S(1)} %subtract_select_fusion.5), channel_id=1, source_target_pairs={{0,32},{8,40},{16,48},{24,56},{32,0},{40,8},{48,16},{56,24},{64,96... | collective-permute-start | bytes 3145736 | tf_op jit(solution)/shard_map/ppermute | solution.py:12
  151.0 22.6 %collective-permute-start.3 = (f32[128,2048]{1,0:T(8,128)S(1)}, f32[128,2048]{1,0:T(8,128)S(1)}, u32[]{:S(2)}, u32[]{:S(2)}) collective-permute-start(f32[128,2048]{1,0:T(8,128)S(1)} %subtract_select_fusion.4), channel_id=1, source_target_pairs={{0,64},{8,72},{16,80},{24,88},{32,96},{40,104},{48,112},{56,120},{... | collective-permute-start | bytes 3145736 | tf_op jit(solution)/shard_map/ppermute | solution.py:12
  173.7 7.0 collective-permute-start.4
  180.8 24.5 %collective-permute-start.5 = (f32[128,2048]{1,0:T(8,128)S(1)}, f32[128,2048]{1,0:T(8,128)S(1)}, u32[]{:S(2)}, u32[]{:S(2)}) collective-permute-start(f32[128,2048]{1,0:T(8,128)S(1)} %subtract_select_fusion.2), channel_id=1, source_target_pairs={{0,2},{1,3},{2,0},{3,1},{4,6},{5,7},{6,4},{7,5},{8,10},{9,11},{10,... | collective-permute-start | bytes 3145736 | tf_op jit(solution)/shard_map/ppermute | solution.py:12
  205.4 25.0 %collective-permute-start.6 = (f32[128,2048]{1,0:T(8,128)S(1)}, f32[128,2048]{1,0:T(8,128)S(1)}, u32[]{:S(2)}, u32[]{:S(2)}) collective-permute-start(f32[128,2048]{1,0:T(8,128)S(1)} %subtract_select_fusion.1), channel_id=1, source_target_pairs={{0,4},{1,5},{2,6},{3,7},{4,0},{5,1},{6,2},{7,3},{8,12},{9,13},{10,... | collective-permute-start | bytes 3145736 | tf_op jit(solution)/shard_map/ppermute | solution.py:12
  247.4 743.8 %all-gather.2.cloned.1.call-start = ((), (), s32[]{:S(2)}) async-start(), calls=%async_computation.1 | async-start | bytes 16908288 | tf_op jit(solution)/shard_map/all_gather | solution.py:55
  1051.0 5.7 copy-start.1
  1108.1 5.7 copy-start
Sparse Core Ops, SparseCore 0:
  247.6 659.1 reduce-scatter.3
  909.9 81.3 all-gather.1
where the time goes:
time: 1580 us; the launch traced here: 1570 us
  waiting for transfers between devices  882 us (56%)
  other arithmetic  377 us (24%)
  matrix products  142 us (9%)
  blocking collectives  68.7 us (4%)
  local copies, waits for them, and re-layouts  61.5 us (4%)
  between operations  25.8 us (2%)
    reduce_scatter x1, waiting for transfers between devices, shards(): lax.psum_scatter(jnp.dot(picked.T, picked, precision=lax.Precision.HIGHES...  659 us
    another operation x62, other arithmetic, shards(): factor = jnp.linalg.cholesky(gram_full)  348 us
    ppermute x7, waiting for transfers between devices, swapped(): return lax.ppermute(value, axis, pairs)  139 us
    another operation x30, matrix products, shards(): factor = jnp.linalg.cholesky(gram_full)  124 us
    all_gather x1, waiting for transfers between devices, shards(): gram_full = lax.all_gather(gram_share, ('fly', 'sub'), axis=0, tiled=True)  83.8 us
    psum x1, blocking collectives, shards(): col_squares = lax.psum(jnp.sum(matrix * matrix, axis=0), ('fly', 'sub'))  68.7 us
  transfers between devices with their start and end apart: 9, of which 9 were waited for; matrix products, arithmetic and copies ran while one was open for 0% of the time, Pallas kernels for 0%

commit v1 on v0

v1 whole, which is shorter than its diff:
```python
import functools
import math

import jax
import jax.numpy as jnp
import numpy as np
from jax import lax
from jax.experimental import pallas as pl
from jax.experimental.pallas import tpu as pltpu
from jax.sharding import PartitionSpec as P

F32 = jnp.float32
BF16 = jnp.bfloat16
BLK = 128
VREG = (8, 128)
AXES = ("fly", "sub")


def sylvester(order):
    idx = np.arange(order)
    common = idx[:, None] & idx[None, :]
    parity = np.zeros((order, order), np.int64)
    for bit in range(order.bit_length() - 1):
        parity ^= common >> bit & 1
    return (1 - 2 * parity).astype(np.float32)


def halves(value):
    high = value.astype(BF16)
    return high, (value - high.astype(F32)).astype(BF16)


def thirds(value):
    high = value.astype(BF16)
    rest = value - high.astype(F32)
    mid = rest.astype(BF16)
    return high, mid, (rest - mid.astype(F32)).astype(BF16)


def contract(a, b, dims):
    return lax.dot_general(a, b, (dims, ((), ())), preferred_element_type=F32)


def contract_split(a, b, dims):
    return contract(a[0], b[0], dims) + (contract(a[0], b[1], dims) + contract(a[1], b[0], dims))


NT = ((1,), (1,))
TN = ((0,), (0,))
NN = ((1,), (0,))


def factor(d_ref, u_ref, inv_ref, cols_ref, rows_ref, irows_ref):
    groups = BLK // 8
    sublane = lax.broadcasted_iota(jnp.int32, VREG, 0)
    lane = lax.broadcasted_iota(jnp.int32, VREG, 1)
    block = [d_ref[8 * g : 8 * g + 8, :] for g in range(groups)]
    inverse = [jnp.where(lane == sublane + 8 * g, 1.0, 0.0).astype(F32) for g in range(groups)]
    for t in range(groups):
        cols = {
            g: [jnp.broadcast_to(block[g][:, 8 * t + c : 8 * t + c + 1], VREG) for c in range(8)]
            for g in range(t, groups)
        }
        cbase, rbase = 64 * (t % 2), 8 * (t % 2)
        for c in range(8):
            cols_ref[cbase + 8 * c : cbase + 8 * c + 8, :] = cols[t][c]
        rows_ref[rbase : rbase + 8, :] = block[t]
        irows_ref[rbase : rbase + 8, :] = inverse[t]
        d = {}
        for k in range(8):
            for i in range(k + 1):
                at = cbase + 8 * k + i
                d[i, k] = jnp.broadcast_to(cols_ref[at : at + 1, :], VREG)
        r = [jnp.broadcast_to(rows_ref[rbase + i : rbase + i + 1, :], VREG) for i in range(8)]
        w = [jnp.broadcast_to(irows_ref[rbase + i : rbase + i + 1, :], VREG) for i in range(8)]
        s, inv, u, v = {}, [None] * 8, [None] * 8, [None] * 8
        for i in range(0, 8, 2):
            a, b, c = d[i, i], d[i, i + 1], d[i + 1, i + 1]
            det = a * c - b * b
            rdet = 1.0 / det
            ra = lax.rsqrt(a)
            l10 = b * ra
            rc = lax.rsqrt(det) * (a * ra)
            inv[i], inv[i + 1] = ra, rc
            s[i, i + 1] = l10
            u[i], v[i] = r[i] * ra, w[i] * ra
            u[i + 1] = (r[i + 1] - l10 * u[i]) * rc
            v[i + 1] = (w[i + 1] - l10 * v[i]) * rc
            later = range(i + 2, 8)
            for k in later:
                s[i, k] = d[i, k] * ra
                s[i + 1, k] = (d[i + 1, k] - l10 * s[i, k]) * rc
            x = {k: c * d[i, k] - b * d[i + 1, k] for k in later}
            y = {k: a * d[i + 1, k] - b * d[i, k] for k in later}
            for k in later:
                for m in range(k, 8):
                    d[k, m] = d[k, m] - (x[k] * d[i, m] + y[k] * d[i + 1, m]) * rdet
                r[k] = r[k] - (s[i, k] * u[i] + s[i + 1, k] * u[i + 1])
                w[k] = w[k] - (s[i, k] * v[i] + s[i + 1, k] * v[i + 1])
        for i in range(8):
            at = 8 * t + i
            u_ref[at : at + 1, :] = u[i][0:1, :]
            inv_ref[at : at + 1, :] = v[i][0:1, :]
        if t == groups - 1:
            break
        q, z = list(u), list(v)
        for i in range(7, -1, -1):
            for k in range(i + 1, 8):
                q[i] = q[i] - s[i, k] * q[k]
                z[i] = z[i] - s[i, k] * z[k]
            q[i], z[i] = q[i] * inv[i], z[i] * inv[i]

        def total(column, row):
            t0 = [column[c] * row[c] for c in range(8)]
            return ((t0[0] + t0[1]) + (t0[2] + t0[3])) + ((t0[4] + t0[5]) + (t0[6] + t0[7]))

        for g in range(t + 1, groups):
            block[g] = block[g] - total(cols[g], q)
            inverse[g] = inverse[g] - total(cols[g], z)


CHUNK = 256


def chol_kernel(
    fly,
    sub,
    place_ref,
    ridge_ref,
    gram_ref,
    out_ref,
    a_ref,
    high_ref,
    rest_ref,
    s_ref,
    d_ref,
    u_ref,
    inv_ref,
    cols_ref,
    rows_ref,
    irows_ref,
    sems,
):
    share, columns = out_ref.shape
    blocks = columns // BLK
    piece = a_ref.shape[0] // (fly * sub)
    stride = piece * fly

    def start(i, _):
        s, f = i // fly, i % fly
        pltpu.make_async_copy(
            gram_ref.at[f * sub + s, pl.ds(0, piece)],
            a_ref.at[pl.ds(pl.multiple_of(i * piece, 8), piece)],
            sems.at[s],
        ).start()
        return 0

    lax.fori_loop(0, fly * sub, start, 0)
    high_ref[...] = jnp.zeros_like(high_ref)
    rest_ref[...] = jnp.zeros_like(rest_ref)
    place = place_ref[0]
    mine = place * share
    mine_block = mine // BLK
    sub_i = lax.broadcasted_iota(jnp.int32, (BLK, BLK), 0)
    lane_i = lax.broadcasted_iota(jnp.int32, (BLK, BLK), 1)
    eye = jnp.where(sub_i == lane_i, ridge_ref[0], 0.0)

    def panel(k, _):
        @pl.when(k < sub)
        def _():
            at = pl.ds(pl.multiple_of(k * stride, 8), stride)
            pltpu.make_async_copy(a_ref.at[at], a_ref.at[at], sems.at[k]).wait()

        other = blocks - 1 - k
        off = jnp.where(k < sub, k * stride, other * stride + (blocks - other) * BLK)
        top = k * BLK
        lanes = pl.ds(pl.multiple_of(top, BLK), BLK)
        mine_rows = pl.ds(pl.multiple_of(top, BLK), BLK)
        depth = pl.cdiv(k * BLK, CHUNK)

        def rows_of(i):
            return pl.ds(pl.multiple_of(top + i * BLK, BLK), BLK)

        def gather(i, _):
            a = a_ref[pl.ds(pl.multiple_of(off + i * BLK, 8), BLK), :]
            at = rows_of(i)

            def step(c, acc):
                cols = pl.ds(pl.multiple_of(c * CHUNK, CHUNK), CHUNK)
                here = high_ref[at, cols], rest_ref[at, cols]
                there = high_ref[mine_rows, cols], rest_ref[mine_rows, cols]
                return acc - contract_split(here, there, NT)

            s_ref[at, :] = lax.fori_loop(0, depth, step, a)
            return 0

        lax.fori_loop(0, blocks - k, gather, 0)
        d_ref[...] = s_ref[mine_rows, :] + eye
        factor(d_ref, u_ref, inv_ref, cols_ref, rows_ref, irows_ref)
        inverse = halves(inv_ref[...])
        s_ref[mine_rows, :] = jnp.where(sub_i >= lane_i, u_ref[...].T, 0.0)

        def solve(i, _):
            at = rows_of(i)
            low = contract_split(halves(s_ref[at, :]), inverse, NT)
            s_ref[at, :] = low
            high, rest = halves(low)
            high_ref[at, lanes] = high
            rest_ref[at, lanes] = rest
            return 0

        lax.fori_loop(1, blocks - k, solve, 0)
        own = s_ref[pl.ds(pl.multiple_of(mine, share), share), :]
        out_ref[:, lanes] = jnp.where(mine_block >= k, own, 0.0)
        return 0

    lax.fori_loop(0, blocks, panel, 0)


def factored(place, ridge, full, fly, sub, share):
    columns = share * fly * sub
    piece = (columns + BLK) // fly
    smem = pl.BlockSpec(memory_space=pltpu.SMEM)
    return pl.pallas_call(
        functools.partial(chol_kernel, fly, sub),
        out_shape=jax.ShapeDtypeStruct((share, columns), F32),
        in_specs=[smem, smem, pl.BlockSpec(memory_space=pl.ANY)],
        scratch_shapes=[
            pltpu.VMEM((piece * fly * sub, BLK), F32),
            pltpu.VMEM((columns, columns), BF16),
            pltpu.VMEM((columns, columns), BF16),
            pltpu.VMEM((columns, BLK), F32),
            pltpu.VMEM((BLK, BLK), F32),
            pltpu.VMEM((BLK, BLK), F32),
            pltpu.VMEM((BLK, BLK), F32),
            pltpu.VMEM((BLK, BLK), F32),
            pltpu.VMEM((16, BLK), F32),
            pltpu.VMEM((16, BLK), F32),
            pltpu.SemaphoreType.DMA((sub,)),
        ],
        compiler_params=pltpu.CompilerParams(vmem_limit_bytes=52 << 20),
        name="cholesky",
    )(place, ridge, full)


def across_kernel(x_ref, table_ref, y_ref, norm_ref):
    devices = table_ref.shape[0]
    per = x_ref.shape[0] // devices
    lanes = lax.broadcasted_iota(jnp.int32, VREG, 1)
    norms = jnp.zeros(VREG, F32)
    total = devices * x_ref.shape[1]
    table = table_ref[...]
    for col in range(per):
        rows = x_ref[pl.ds(col, devices, stride=per), :]
        squares = jnp.sum(jnp.sum(rows * rows, axis=0, keepdims=True), axis=1, keepdims=True)
        norm = jnp.sqrt(jnp.broadcast_to(squares, VREG) / total + 1e-06)
        norms = jnp.where(lanes == col, norm, norms)
        scale = 1.0 / (norm[0:1, :] * math.sqrt(total))
        high, mid, low = thirds(rows)
        mixed = contract(table, high, NN) + (contract(table, mid, NN) + contract(table, low, NN))
        y_ref[pl.ds(col, devices, stride=per), :] = mixed * scale
    norm_ref[...] = norms


def across(x, table):
    return pl.pallas_call(
        across_kernel,
        out_shape=[jax.ShapeDtypeStruct(x.shape, F32), jax.ShapeDtypeStruct(VREG, F32)],
        compiler_params=pltpu.CompilerParams(vmem_limit_bytes=32 << 20),
        name="across_devices",
    )(x, table)


def gram_kernel(sub_ref, *refs):
    picks, out_ref, high_ref, rest_ref = refs[:-3], refs[-3], refs[-2], refs[-1]
    sub = sub_ref[0]
    samples, columns = picks[0].shape
    blocks = columns // BLK
    for i, ref in enumerate(picks):
        high, rest = halves(ref[...])
        high_ref[i * samples : (i + 1) * samples, :] = high
        rest_ref[i * samples : (i + 1) * samples, :] = rest

    def block(index):
        at = pl.ds(pl.multiple_of(index * BLK, BLK), BLK)
        return high_ref[:, at], rest_ref[:, at]

    for j in range(blocks + 1):
        first = j < blocks - sub
        row = jnp.where(first, sub + j, j - 1)
        col = jnp.where(first, sub, blocks - 1 - sub)
        out_ref[j * BLK : (j + 1) * BLK, :] = contract_split(block(row), block(col), TN)


def gram_share(sub, picks):
    samples, columns = picks[0].shape
    rows = samples * len(picks)
    return pl.pallas_call(
        gram_kernel,
        out_shape=jax.ShapeDtypeStruct((columns + BLK, BLK), F32),
        in_specs=[pl.BlockSpec(memory_space=pltpu.SMEM)]
        + [pl.BlockSpec(memory_space=pltpu.VMEM)] * len(picks),
        scratch_shapes=[pltpu.VMEM((rows, columns), BF16)] * 2,
        compiler_params=pltpu.CompilerParams(vmem_limit_bytes=32 << 20),
        name="gram_share",
    )(sub, *picks)


def shards(matrix, row_signs, sample_idx, ridge_shift):
    rows_here, columns = matrix.shape
    fly, sub = lax.axis_size("fly"), lax.axis_size("sub")
    devices = fly * sub
    place = lax.axis_index(AXES)
    samples_all = sample_idx.shape[0] * devices
    per = columns // devices
    signed = (matrix * row_signs.astype(F32)[:, None]).T
    spread = lax.all_to_all(signed.reshape(devices, per, rows_here), AXES, 0, 0, tiled=True)
    table = jnp.asarray(sylvester(devices), BF16)
    mixed, norms = across(spread.reshape(columns, rows_here), table)
    back = lax.all_to_all(mixed.reshape(devices, per, rows_here), AXES, 0, 0, tiled=True)
    chosen = jnp.take(jnp.asarray(sylvester(rows_here)), sample_idx, axis=0)
    picked = lax.dot_general(
        chosen,
        back.reshape(columns, rows_here),
        (NT, ((), ())),
        precision=lax.Precision.HIGHEST,
        preferred_element_type=F32,
    )
    picks = [picked]
    for step in range(1, sub):
        picks.append(lax.ppermute(picked, "sub", [(i, (i + step) % sub) for i in range(sub)]))
    share = gram_share(lax.axis_index("sub").astype(jnp.int32)[None], picks)
    piece = (columns + BLK) // fly
    parts = lax.all_to_all(share.reshape(fly, piece, BLK), "fly", 0, 0, tiled=True)
    summed = jnp.sum(parts, axis=0) / samples_all
    full = lax.all_gather(jnp.concatenate([summed, norms], axis=0), AXES)
    chol = factored(place.astype(jnp.int32)[None], ridge_shift, full, fly, sub, per)
    col_norms = full[:, piece, :per].reshape(columns)
    return (chol, col_norms)


def solution(mesh):
    in_specs = (P(AXES, None), P(AXES), P(AXES), P())
    out_specs = (P(AXES, None), P())
    return jax.shard_map(shards, mesh=mesh, in_specs=in_specs, out_specs=out_specs, check_vma=False)
```

time: 1580 us -> 375 us (0.24)
  waiting for transfers between devices: 882 us -> 108 us
  other arithmetic: 377 us -> 1.46 us
  Pallas kernels: 0 us -> 182 us
  matrix products: 142 us -> 1.19 us
  local copies, waits for them, and re-layouts: 61.5 us -> 4.82 us
  blocking collectives: 68.7 us -> 49.7 us
    reduce_scatter x1 -> x0, waiting for transfers between devices: 659 us -> none  [shards(): lax.psum_scatter(jnp.dot(picked.T, picked, precision=lax.Precision.HIGHES...]
    another operation x62 -> x0, other arithmetic: 348 us -> none  [shards(): factor = jnp.linalg.cholesky(gram_full)]
    pallas_call x0 -> x3, Pallas kernels: none -> 182 us  [the longest x1 178 us: factored(): pl.pallas_call(functools.partial(chol_kernel, fly, sub), out_shape=jax.Sh...]
    another operation x30 -> x0, matrix products: 124 us -> none  [shards(): factor = jnp.linalg.cholesky(gram_full)]
    ppermute x7, waiting for transfers between devices: 139 us -> 23.1 us  [shards(): lax.ppermute(picked, 'sub', [(i, (i + step) % sub) for i in range(sub)])]
    psum x1 -> x0, blocking collectives: 68.7 us -> none  [shards(): col_squares = lax.psum(jnp.sum(matrix * matrix, axis=0), ('fly', 'sub'))]
    all_to_all x0 -> x2, blocking collectives: none -> 49.7 us  [the longest x1 30.6 us: shards(): lax.all_to_all(signed.reshape(devices, per, rows_here), AXES, 0, 0, tiled...]
    all_to_all x0 -> x1, waiting for transfers between devices: none -> 18.8 us  [shards(): lax.all_to_all(mixed.reshape(devices, per, rows_here), AXES, 0, 0, tiled=...]
  transfers between devices with their start and end apart: 9 -> 9, of which waited for: 9 -> 5; matrix products, arithmetic and copies ran while one was open for 0% -> 0% of each run, Pallas kernels for 0% -> 0%
where the time goes in v1:
time: 375 us
  Pallas kernels  182 us (49%)
  waiting for transfers between devices  108 us (29%)
  blocking collectives  49.7 us (13%)
  between operations  14.8 us (4%)
  starting transfers between devices  13.3 us (4%)
  local copies, waits for them, and re-layouts  4.82 us (1%)
    pallas_call x1, Pallas kernels, factored(): pl.pallas_call(functools.partial(chol_kernel, fly, sub), out_shape=jax.Sh...  178 us
    all_gather x1, waiting for transfers between devices, shards(): full = lax.all_gather(jnp.concatenate([summed, norms], axis=0), AXES)  65.7 us
    all_to_all x1, blocking collectives, shards(): lax.all_to_all(signed.reshape(devices, per, rows_here), AXES, 0, 0, tiled...  30.6 us
    ppermute x7, waiting for transfers between devices, shards(): lax.ppermute(picked, 'sub', [(i, (i + step) % sub) for i in range(sub)])  23.1 us
    all_to_all x1, blocking collectives, shards(): lax.all_to_all(share.reshape(fly, piece, BLK), 'fly', 0, 0, tiled=True)  19 us
    all_to_all x1, waiting for transfers between devices, shards(): lax.all_to_all(mixed.reshape(devices, per, rows_here), AXES, 0, 0, tiled=...  18.8 us
    ppermute x7, starting transfers between devices, shards(): lax.ppermute(picked, 'sub', [(i, (i + step) % sub) for i in range(sub)])  8.96 us
  transfers between devices with their start and end apart: 9, of which 5 were waited for; matrix products, arithmetic and copies ran while one was open for 0% of the time, Pallas kernels for 0%

profile of v1, /device:TPU:1, one launch (start us, length us, event | category | flops | bytes accessed | tf_op | source)
XLA Modules:
  0.0 374.9 jit_solution(18089264775658679612)
XLA Ops:
  7.2 0.0 copy-start.1
  7.2 0.0 copy-start.2
  7.2 1.6 copy.9
  8.8 0.7 convert_element_type.3
  9.4 0.1 broadcast_multiply_fusion
  9.5 30.6 %all_to_all.15 = f32[128,16,128]{2,1,0:T(8,128)S(1)} all-to-all(f32[128,16,128]{2,1,0:T(8,128)S(1)} %bitcast.15), channel_id=1, replica_groups=mesh['fly'=16,'sub'=8] {'fly','sub'}, dimensions={0} | all-to-all | bytes 2097152 | tf_op jit(solution)/shard_map/all_to_all | solution.py:317
  40.2 0.0 copy-start
  40.2 0.8 copy-done
  40.9 2.0 across_devices.1
  42.9 4.3 %all-to-all-start.1 = ((f32[128,16,128]{2,1,0:T(8,128)}), f32[128,16,128]{2,1,0:T(8,128)S(1)}, u32[]{:S(2)}, u32[]{:S(2)}) async-start(f32[128,16,128]{2,1,0:T(8,128)} %bitcast.5), calls=%async_computation.1 | async-start | bytes 2097152 | tf_op jit(solution)/shard_map/all_to_all | solution.py:320
  47.3 0.0 all-gather.3.cloned.1.call-start
  47.3 0.0 copy-done.2
  47.4 0.0 copy-done.1
  47.4 0.6 gather_fusion
  48.0 18.8 %all-to-all-done.1 = f32[128,16,128]{2,1,0:T(8,128)S(1)} async-done(((f32[128,16,128]{2,1,0:T(8,128)}), f32[128,16,128]{2,1,0:T(8,128)S(1)}, u32[]{:S(2)}, u32[]{:S(2)}) %all-to-all-start.1) | async-done | bytes 1048608 | tf_op jit(solution)/shard_map/all_to_all | solution.py:320
  66.7 1.2 fusion.refs_0_
  67.9 1.1 collective-permute-start
  69.0 0.0 collective-permute-start.1
  69.0 1.7 collective-permute-start.2
  70.7 1.9 collective-permute-start.3
  72.6 2.6 collective-permute-start.4
  75.2 0.0 collective-permute-done.refs_1_
  75.2 1.7 collective-permute-start.5
  76.9 17.3 %collective-permute-done.1.refs_2_ = f32[32,2048]{1,0:T(8,128)S(1)} collective-permute-done((f32[32,2048]{1,0:T(8,128)S(1)}, f32[32,2048]{1,0:T(8,128)S(1)}, u32[]{:S(2)}, u32[]{:S(2)}) %collective-permute-start.1) | collective-permute-done | bytes 262176 | tf_op jit(solution)/shard_map/ppermute | solution.py:331
  94.2 0.0 collective-permute-start.6
  94.2 0.6 collective-permute-done.2.refs_3_
  94.8 0.0 collective-permute-done.3.refs_4_
  94.8 0.0 collective-permute-done.4.refs_5_
  94.8 0.0 collective-permute-done.5.refs_6_
  94.8 5.2 %collective-permute-done.6.refs_7_ = f32[32,2048]{1,0:T(8,128)S(1)} collective-permute-done((f32[32,2048]{1,0:T(8,128)S(1)}, f32[32,2048]{1,0:T(8,128)S(1)}, u32[]{:S(2)}, u32[]{:S(2)}) %collective-permute-start.6) | collective-permute-done | bytes 262176 | tf_op jit(solution)/shard_map/ppermute | solution.py:331
  100.0 1.9 gram_share.1
  101.9 19.0 %all_to_all.16 = f32[16,136,128]{2,1,0:T(8,128)S(1)} all-to-all(f32[16,136,128]{2,1,0:T(8,128)S(1)} %bitcast.11), channel_id=1, replica_groups=mesh['fly'=16,'sub'=8] {'fly'}, dimensions={0} | all-to-all | bytes 2228224 | tf_op jit(solution)/shard_map/all_to_all | solution.py:334
  120.9 0.1 reduce_sum.9
  121.0 0.6 pad_maximum_fusion
  121.6 0.0 all-gather.3.cloned.1.call-update
  122.3 65.7 %all-gather.3.cloned.1.call-done = f32[18432,128]{1,0:T(8,128)} async-done(((f32[144,128]{1,0:T(8,128)}), f32[18432,128]{1,0:T(8,128)}) %all-gather.3.cloned.1.call-update) | async-done | bytes 9437200 | tf_op jit(solution)/shard_map/all_gather | solution.py:336
  188.0 1.2 slice_reduce_fusion
  189.2 0.7 reshape_squeeze.3
  189.9 178.2 %cholesky.1 = f32[16,2048]{1,0:T(8,128)} custom-call(s32[1]{0:T(128)} %bitcast.place_ref, f32[1]{0:T(128)S(6)} %copy.10.ridge_ref, f32[128,144,128]{2,1,0:T(8,128)} %bitcast.14), custom_call_target="tpu_custom_call" | custom-call | tf_op jit(solution)/shard_map/cholesky/pallas_call | solution.py:224
  (4 shorter events, 0.0 us)
Async XLA Ops:
  7.2 40.2 %copy-start.1 = (f32[128,128]{1,0:T(8,128)S(1)}, f32[128,128]{1,0:T(8,128)}, u32[]{:S(2)}) copy-start(f32[128,128]{1,0:T(8,128)} %constant.37.clone) | copy-start | bytes 196612
  7.2 40.2 %copy-start.2 = (s32[32]{0:T(128)S(1)}, s32[32]{0:T(128)}, u32[]{:S(2)}) copy-start(s32[32]{0:T(128)} %param.8) | copy-start | bytes 388
  40.2 0.8 copy-start
  42.9 23.8 %all-to-all-start.1 = ((f32[128,16,128]{2,1,0:T(8,128)}), f32[128,16,128]{2,1,0:T(8,128)S(1)}, u32[]{:S(2)}, u32[]{:S(2)}) async-start(f32[128,16,128]{2,1,0:T(8,128)} %bitcast.5), calls=%async_computation.1 | async-start | bytes 2097152 | tf_op jit(solution)/shard_map/all_to_all | solution.py:320
  47.3 140.7 %all-gather.3.cloned.1.call-start = ((), (), s32[]{:S(2)}) async-start(), calls=%async_computation.3 | async-start | bytes 9510912 | tf_op jit(solution)/shard_map/all_gather | solution.py:336
  67.9 7.3 %collective-permute-start = (f32[32,2048]{1,0:T(8,128)S(1)}, f32[32,2048]{1,0:T(8,128)S(1)}, u32[]{:S(2)}, u32[]{:S(2)}) collective-permute-start(f32[32,2048]{1,0:T(8,128)S(1)} %fusion.refs_0_), channel_id=1, source_target_pairs={{0,1},{1,2},{2,3},{3,4},{4,5},{5,6},{6,7},{7,0},{8,9},{9,10},{10,1... | collective-permute-start | bytes 786440 | tf_op jit(solution)/shard_map/ppermute | solution.py:331
  69.0 25.2 %collective-permute-start.1 = (f32[32,2048]{1,0:T(8,128)S(1)}, f32[32,2048]{1,0:T(8,128)S(1)}, u32[]{:S(2)}, u32[]{:S(2)}) collective-permute-start(f32[32,2048]{1,0:T(8,128)S(1)} %fusion.refs_0_), channel_id=1, source_target_pairs={{0,2},{1,3},{2,4},{3,5},{4,6},{5,7},{6,0},{7,1},{8,10},{9,11},{10,... | collective-permute-start | bytes 786440 | tf_op jit(solution)/shard_map/ppermute | solution.py:331
  69.0 25.8 %collective-permute-start.2 = (f32[32,2048]{1,0:T(8,128)S(1)}, f32[32,2048]{1,0:T(8,128)S(1)}, u32[]{:S(2)}, u32[]{:S(2)}) collective-permute-start(f32[32,2048]{1,0:T(8,128)S(1)} %fusion.refs_0_), channel_id=1, source_target_pairs={{0,3},{1,4},{2,5},{3,6},{4,7},{5,0},{6,1},{7,2},{8,11},{9,12},{10,... | collective-permute-start | bytes 786440 | tf_op jit(solution)/shard_map/ppermute | solution.py:331
  70.7 24.1 %collective-permute-start.3 = (f32[32,2048]{1,0:T(8,128)S(1)}, f32[32,2048]{1,0:T(8,128)S(1)}, u32[]{:S(2)}, u32[]{:S(2)}) collective-permute-start(f32[32,2048]{1,0:T(8,128)S(1)} %fusion.refs_0_), channel_id=1, source_target_pairs={{0,4},{1,5},{2,6},{3,7},{4,0},{5,1},{6,2},{7,3},{8,12},{9,13},{10,... | collective-permute-start | bytes 786440 | tf_op jit(solution)/shard_map/ppermute | solution.py:331
  72.6 22.2 %collective-permute-start.4 = (f32[32,2048]{1,0:T(8,128)S(1)}, f32[32,2048]{1,0:T(8,128)S(1)}, u32[]{:S(2)}, u32[]{:S(2)}) collective-permute-start(f32[32,2048]{1,0:T(8,128)S(1)} %fusion.refs_0_), channel_id=1, source_target_pairs={{0,5},{1,6},{2,7},{3,0},{4,1},{5,2},{6,3},{7,4},{8,13},{9,14},{10,... | collective-permute-start | bytes 786440 | tf_op jit(solution)/shard_map/ppermute | solution.py:331
  75.2 19.6 %collective-permute-start.5 = (f32[32,2048]{1,0:T(8,128)S(1)}, f32[32,2048]{1,0:T(8,128)S(1)}, u32[]{:S(2)}, u32[]{:S(2)}) collective-permute-start(f32[32,2048]{1,0:T(8,128)S(1)} %fusion.refs_0_), channel_id=1, source_target_pairs={{0,6},{1,7},{2,0},{3,1},{4,2},{5,3},{6,4},{7,5},{8,14},{9,15},{10,... | collective-permute-start | bytes 786440 | tf_op jit(solution)/shard_map/ppermute | solution.py:331
  94.2 5.8 %collective-permute-start.6 = (f32[32,2048]{1,0:T(8,128)S(1)}, f32[32,2048]{1,0:T(8,128)S(1)}, u32[]{:S(2)}, u32[]{:S(2)}) collective-permute-start(f32[32,2048]{1,0:T(8,128)S(1)} %fusion.refs_0_), channel_id=1, source_target_pairs={{0,7},{1,0},{2,1},{3,2},{4,3},{5,4},{6,5},{7,6},{8,15},{9,8},{10,9... | collective-permute-start | bytes 786440 | tf_op jit(solution)/shard_map/ppermute | solution.py:331
Sparse Core Ops, SparseCore 0:
  121.8 66.1 all-gather.2

commit v2 on v1

--- a/solution.py
+++ b/solution.py
@@ -48,78 +48,91 @@
 NT = ((1,), (1,))
 TN = ((0,), (0,))
 NN = ((1,), (0,))
-
-
-def factor(d_ref, u_ref, inv_ref, cols_ref, rows_ref, irows_ref):
-    groups = BLK // 8
+WIDE = 16
+
+
+def factor(d_ref, u_ref, inv_ref):
+    steps, tall = BLK // WIDE, WIDE // 8
     sublane = lax.broadcasted_iota(jnp.int32, VREG, 0)
     lane = lax.broadcasted_iota(jnp.int32, VREG, 1)
+    groups = BLK // 8
     block = [d_ref[8 * g : 8 * g + 8, :] for g in range(groups)]
     inverse = [jnp.where(lane == sublane + 8 * g, 1.0, 0.0).astype(F32) for g in range(groups)]
-    for t in range(groups):
-        cols = {
-            g: [jnp.broadcast_to(block[g][:, 8 * t + c : 8 * t + c + 1], VREG) for c in range(8)]
-            for g in range(t, groups)
-        }
-        cbase, rbase = 64 * (t % 2), 8 * (t % 2)
-        for c in range(8):
-            cols_ref[cbase + 8 * c : cbase + 8 * c + 8, :] = cols[t][c]
-        rows_ref[rbase : rbase + 8, :] = block[t]
-        irows_ref[rbase : rbase + 8, :] = inverse[t]
-        d = {}
-        for k in range(8):
-            for i in range(k + 1):
-                at = cbase + 8 * k + i
-                d[i, k] = jnp.broadcast_to(cols_ref[at : at + 1, :], VREG)
-        r = [jnp.broadcast_to(rows_ref[rbase + i : rbase + i + 1, :], VREG) for i in range(8)]
-        w = [jnp.broadcast_to(irows_ref[rbase + i : rbase + i + 1, :], VREG) for i in range(8)]
-        s, inv, u, v = {}, [None] * 8, [None] * 8, [None] * 8
-        for i in range(0, 8, 2):
-            a, b, c = d[i, i], d[i, i + 1], d[i + 1, i + 1]
+
+    def row(parts, i):
+        part = parts[i // 8]
+        return jnp.broadcast_to(part[i % 8 : i % 8 + 1, :], VREG)
+
+    def total(terms):
+        while len(terms) > 1:
+            terms = [terms[i] + terms[i + 1] for i in range(0, len(terms), 2)]
+        return terms[0]
+
+    for t in range(steps):
+        first = t * tall
+
+        def column(g, c):
+            at = WIDE * t + c
+            return jnp.broadcast_to(block[g][:, at : at + 1], VREG)
+
+        mine = range(first, first + tall)
+        cols = [[column(g, c) for g in mine] for c in range(WIDE)]
+        raw = [block[g] for g in mine]
+        r, w = list(raw), [inverse[g] for g in mine]
+        after = range(first + tall, min(first + 2 * tall, groups))
+        ahead = {g: [column(g, c) for c in range(WIDE)] for g in after}
+        for i in range(0, WIDE, 2):
+            v, lo = i // 8, i % 8
+            is_i, is_j = sublane == lo, sublane == lo + 1
+            pair = jnp.logical_or(is_i, is_j)
+            a, b, c = row(cols[i], i), row(cols[i + 1], i), row(cols[i + 1], i + 1)
             det = a * c - b * b
             rdet = 1.0 / det
             ra = lax.rsqrt(a)
             l10 = b * ra
             rc = lax.rsqrt(det) * (a * ra)
-            inv[i], inv[i + 1] = ra, rc
-            s[i, i + 1] = l10
-            u[i], v[i] = r[i] * ra, w[i] * ra
-            u[i + 1] = (r[i + 1] - l10 * u[i]) * rc
-            v[i + 1] = (w[i + 1] - l10 * v[i]) * rc
-            later = range(i + 2, 8)
-            for k in later:
-                s[i, k] = d[i, k] * ra
-                s[i + 1, k] = (d[i + 1, k] - l10 * s[i, k]) * rc
-            x = {k: c * d[i, k] - b * d[i + 1, k] for k in later}
-            y = {k: a * d[i + 1, k] - b * d[i, k] for k in later}
-            for k in later:
-                for m in range(k, 8):
-                    d[k, m] = d[k, m] - (x[k] * d[i, m] + y[k] * d[i + 1, m]) * rdet
-                r[k] = r[k] - (s[i, k] * u[i] + s[i + 1, k] * u[i + 1])
-                w[k] = w[k] - (s[i, k] * v[i] + s[i + 1, k] * v[i + 1])
-        for i in range(8):
-            at = 8 * t + i
-            u_ref[at : at + 1, :] = u[i][0:1, :]
-            inv_ref[at : at + 1, :] = v[i][0:1, :]
-        if t == groups - 1:
+            x = [c * p - b * q for p, q in zip(cols[i], cols[i + 1])]
+            y = [a * q - b * p for p, q in zip(cols[i], cols[i + 1])]
+            x[v] = jnp.where(is_i, -c, jnp.where(is_j, b, x[v]))
+            y[v] = jnp.where(is_i, b, jnp.where(is_j, -a, y[v]))
+
+            def sweep(parts):
+                ri, rj = row(parts, i), row(parts, i + 1)
+                out = []
+                for n, part in enumerate(parts):
+                    z = (x[n] * ri + y[n] * rj) * rdet
+                    out.append((jnp.where(pair, 0.0, part) if n == v else part) - z)
+                return out
+
+            for m in range(i + 2, WIDE):
+                cols[m] = sweep(cols[m])
+            at = WIDE * t + i
+            for parts, ref in ((r, u_ref), (w, inv_ref)):
+                ui = row(parts, i) * ra
+                uj = (row(parts, i + 1) - l10 * ui) * rc
+                ref[at : at + 1, :] = ui[0:1]
+                ref[at + 1 : at + 2, :] = uj[0:1]
+            r, w = sweep(r), sweep(w)
+        if t == steps - 1:
             break
-        q, z = list(u), list(v)
-        for i in range(7, -1, -1):
-            for k in range(i + 1, 8):
-                q[i] = q[i] - s[i, k] * q[k]
-                z[i] = z[i] - s[i, k] * z[k]
-            q[i], z[i] = q[i] * inv[i], z[i] * inv[i]
-
-        def total(column, row):
-            t0 = [column[c] * row[c] for c in range(8)]
-            return ((t0[0] + t0[1]) + (t0[2] + t0[3])) + ((t0[4] + t0[5]) + (t0[6] + t0[7]))
-
-        for g in range(t + 1, groups):
-            block[g] = block[g] - total(cols[g], q)
-            inverse[g] = inverse[g] - total(cols[g], z)
-
-
-CHUNK = 256
+        q = [row(r, c) for c in range(WIDE)]
+        z = [row(w, c) for c in range(WIDE)]
+        for g in after:
+            block[g] = block[g] - total([ahead[g][c] * q[c] for c in range(WIDE)])
+            inverse[g] = inverse[g] - total([ahead[g][c] * z[c] for c in range(WIDE)])
+        if t + 2 < steps:
+            xh, xm, xl = [p.astype(F32) for p in thirds(jnp.concatenate(raw, axis=0))]
+            solved = jnp.concatenate([jnp.concatenate(r, axis=0), jnp.concatenate(w, axis=0)], axis=1)
+            yh, ym, yl = [p.astype(F32) for p in thirds(solved)]
+            left = jnp.concatenate([xh, xm, xh, xm, xl, xh], axis=0).astype(BF16)
+            right = jnp.concatenate([yh, yh, ym, ym, yh, yl], axis=0).astype(BF16)
+            update = contract(left, right, TN)
+            for g in range(first + 2 * tall, groups):
+                block[g] = block[g] - update[8 * g : 8 * g + 8, :BLK]
+                inverse[g] = inverse[g] - update[8 * g : 8 * g + 8, BLK:]
+
+
+SPAN = 4
 
 
 def chol_kernel(
@@ -136,15 +149,14 @@
     d_ref,
     u_ref,
     inv_ref,
-    cols_ref,
-    rows_ref,
-    irows_ref,
     sems,
 ):
     share, columns = out_ref.shape
     blocks = columns // BLK
     piece = a_ref.shape[0] // (fly * sub)
     stride = piece * fly
+    wide = SPAN * BLK
+    spans = blocks // SPAN
 
     def start(i, _):
         s, f = i // fly, i % fly
@@ -156,65 +168,78 @@
         return 0
 
     lax.fori_loop(0, fly * sub, start, 0)
-    high_ref[...] = jnp.zeros_like(high_ref)
-    rest_ref[...] = jnp.zeros_like(rest_ref)
-    place = place_ref[0]
-    mine = place * share
-    mine_block = mine // BLK
+    arrived = set()
     sub_i = lax.broadcasted_iota(jnp.int32, (BLK, BLK), 0)
     lane_i = lax.broadcasted_iota(jnp.int32, (BLK, BLK), 1)
     eye = jnp.where(sub_i == lane_i, ridge_ref[0], 0.0)
 
-    def panel(k, _):
-        @pl.when(k < sub)
-        def _():
-            at = pl.ds(pl.multiple_of(k * stride, 8), stride)
-            pltpu.make_async_copy(a_ref.at[at], a_ref.at[at], sems.at[k]).wait()
-
+    def offset(k):
         other = blocks - 1 - k
-        off = jnp.where(k < sub, k * stride, other * stride + (blocks - other) * BLK)
-        top = k * BLK
-        lanes = pl.ds(pl.multiple_of(top, BLK), BLK)
-        mine_rows = pl.ds(pl.multiple_of(top, BLK), BLK)
-        depth = pl.cdiv(k * BLK, CHUNK)
-
-        def rows_of(i):
-            return pl.ds(pl.multiple_of(top + i * BLK, BLK), BLK)
-
-        def gather(i, _):
-            a = a_ref[pl.ds(pl.multiple_of(off + i * BLK, 8), BLK), :]
-            at = rows_of(i)
-
-            def step(c, acc):
-                cols = pl.ds(pl.multiple_of(c * CHUNK, CHUNK), CHUNK)
-                here = high_ref[at, cols], rest_ref[at, cols]
-                there = high_ref[mine_rows, cols], rest_ref[mine_rows, cols]
-                return acc - contract_split(here, there, NT)
-
-            s_ref[at, :] = lax.fori_loop(0, depth, step, a)
+        return k * stride if k < sub else other * stride + (blocks - other) * BLK
+
+    for q in range(spans):
+        left = q * wide
+        for j in range(SPAN):
+            k = q * SPAN + j
+            owner = min(k, blocks - 1 - k)
+            if owner not in arrived:
+                arrived.add(owner)
+                at = pl.ds(owner * stride, stride)
+                pltpu.make_async_copy(a_ref.at[at], a_ref.at[at], sems.at[owner]).wait()
+        for top in range(left, columns, wide):
+            rows = slice(top, top + wide)
+            if q:
+                here = high_ref[rows, :left], rest_ref[rows, :left]
+                there = high_ref[left : left + wide, :left], rest_ref[left : left + wide, :left]
+                known = contract_split(here, there, NT)
+            for j in range(SPAN):
+                k = q * SPAN + j
+                skip = j * BLK if top == left else 0
+                lanes = slice(j * BLK, (j + 1) * BLK)
+                at = offset(k) + top + skip - k * BLK
+                value = a_ref[at : at + wide - skip, :]
+                if q:
+                    value = value - known[skip:, lanes]
+                s_ref[top + skip : top + wide, lanes] = value
+
+        def panel(j, _):
+            top = pl.multiple_of(left + j * BLK, BLK)
+            mine = pl.ds(top, BLK)
+            here = pl.ds(pl.multiple_of(j * BLK, BLK), BLK)
+            there = pl.ds(top, BLK)
+            for depth in range(1, SPAN):
+
+                @pl.when(j == depth)
+                def _():
+                    lanes = slice(depth * BLK, (depth + 1) * BLK)
+                    cols = slice(left, left + depth * BLK)
+                    at = left + depth * BLK
+                    own = high_ref[at : at + BLK, cols], rest_ref[at : at + BLK, cols]
+                    for first in range(left, columns, wide):
+                        rows = slice(max(first, at), first + wide)
+                        part = high_ref[rows, cols], rest_ref[rows, cols]
+                        s_ref[rows, lanes] = s_ref[rows, lanes] - contract_split(part, own, NT)
+
+            d_ref[...] = s_ref[mine, here] + eye
+            factor(d_ref, u_ref, inv_ref)
+            inverse = halves(inv_ref[...])
+            for first in range(left, columns, wide):
+                rows = slice(first, first + wide)
+                high, rest = halves(contract_split(halves(s_ref[rows, here]), inverse, NT))
+                high_ref[rows, there] = high
+                rest_ref[rows, there] = rest
+            high, rest = halves(u_ref[...].T)
+            high_ref[mine, there] = high
+            rest_ref[mine, there] = rest
             return 0
 
-        lax.fori_loop(0, blocks - k, gather, 0)
-        d_ref[...] = s_ref[mine_rows, :] + eye
-        factor(d_ref, u_ref, inv_ref, cols_ref, rows_ref, irows_ref)
-        inverse = halves(inv_ref[...])
-        s_ref[mine_rows, :] = jnp.where(sub_i >= lane_i, u_ref[...].T, 0.0)
-
-        def solve(i, _):
-            at = rows_of(i)
-            low = contract_split(halves(s_ref[at, :]), inverse, NT)
-            s_ref[at, :] = low
-            high, rest = halves(low)
-            high_ref[at, lanes] = high
-            rest_ref[at, lanes] = rest
-            return 0
-
-        lax.fori_loop(1, blocks - k, solve, 0)
-        own = s_ref[pl.ds(pl.multiple_of(mine, share), share), :]
-        out_ref[:, lanes] = jnp.where(mine_block >= k, own, 0.0)
-        return 0
-
-    lax.fori_loop(0, blocks, panel, 0)
+        lax.fori_loop(0, SPAN, panel, 0)
+    mine = place_ref[0] * share
+    at = pl.ds(pl.multiple_of(mine, share), share)
+    row = lax.broadcasted_iota(jnp.int32, (share, columns), 0) + mine
+    col = lax.broadcasted_iota(jnp.int32, (share, columns), 1)
+    value = high_ref[at, :].astype(F32) + rest_ref[at, :].astype(F32)
+    out_ref[...] = jnp.where(col <= row, value, 0.0)
 
 
 def factored(place, ridge, full, fly, sub, share):
@@ -229,13 +254,10 @@
             pltpu.VMEM((piece * fly * sub, BLK), F32),
             pltpu.VMEM((columns, columns), BF16),
             pltpu.VMEM((columns, columns), BF16),
-            pltpu.VMEM((columns, BLK), F32),
+            pltpu.VMEM((columns, SPAN * BLK), F32),
             pltpu.VMEM((BLK, BLK), F32),
             pltpu.VMEM((BLK, BLK), F32),
             pltpu.VMEM((BLK, BLK), F32),
-            pltpu.VMEM((BLK, BLK), F32),
-            pltpu.VMEM((16, BLK), F32),
-            pltpu.VMEM((16, BLK), F32),
             pltpu.SemaphoreType.DMA((sub,)),
         ],
         compiler_params=pltpu.CompilerParams(vmem_limit_bytes=52 << 20),
@@ -327,8 +349,9 @@
         preferred_element_type=F32,
     )
     picks = [picked]
-    for step in range(1, sub):
+    for step in range(2, sub, 2):
         picks.append(lax.ppermute(picked, "sub", [(i, (i + step) % sub) for i in range(sub)]))
+    picks += [lax.ppermute(value, "sub", [(i, i ^ 1) for i in range(sub)]) for value in picks]
     share = gram_share(lax.axis_index("sub").astype(jnp.int32)[None], picks)
     piece = (columns + BLK) // fly
     parts = lax.all_to_all(share.reshape(fly, piece, BLK), "fly", 0, 0, tiled=True)

time: 375 us -> 256 us (0.68)
  Pallas kernels: 182 us -> 73.5 us
  waiting for transfers between devices: 108 us -> 94.3 us
    pallas_call x1, Pallas kernels: 178 us -> 69.6 us  [factored(): pl.pallas_call(functools.partial(chol_kernel, fly, sub), out_shape=jax.Sh...]
    ppermute x7 -> x3, waiting for transfers between devices: 23.1 us -> 5.34 us  [shards(): lax.ppermute(picked, 'sub', [(i, (i + step) % sub) for i in range(sub)])]
    ppermute x0 -> x4, starting transfers between devices: none -> 8.15 us  [shards(): lax.ppermute(value, 'sub', [(i, i ^ 1) for i in range(sub)])]
    ppermute x7 -> x3, starting transfers between devices: 8.96 us -> 2.74 us  [shards(): lax.ppermute(picked, 'sub', [(i, (i + step) % sub) for i in range(sub)])]
  transfers between devices with their start and end apart: 9 -> 9, of which waited for: 5 -> 6; matrix products, arithmetic and copies ran while one was open for 0% -> 0% of each run, Pallas kernels for 0% -> 0%
where the time goes in v2:
time: 256 us
  waiting for transfers between devices  94.3 us (37%)
  Pallas kernels  73.5 us (29%)
  blocking collectives  50.4 us (20%)
  starting transfers between devices  15.3 us (6%)
  between operations  14.8 us (6%)
  local copies, waits for them, and re-layouts  4.82 us (2%)
    pallas_call x1, Pallas kernels, factored(): pl.pallas_call(functools.partial(chol_kernel, fly, sub), out_shape=jax.Sh...  69.6 us
    all_gather x1, waiting for transfers between devices, shards(): full = lax.all_gather(jnp.concatenate([summed, norms], axis=0), AXES)  68.9 us
    all_to_all x1, blocking collectives, shards(): lax.all_to_all(signed.reshape(devices, per, rows_here), AXES, 0, 0, tiled...  30.6 us
    all_to_all x1, blocking collectives, shards(): lax.all_to_all(share.reshape(fly, piece, BLK), 'fly', 0, 0, tiled=True)  19.7 us
    all_to_all x1, waiting for transfers between devices, shards(): lax.all_to_all(mixed.reshape(devices, per, rows_here), AXES, 0, 0, tiled=...  18.8 us
    ppermute x4, starting transfers between devices, shards(): lax.ppermute(value, 'sub', [(i, i ^ 1) for i in range(sub)])  8.15 us
    ppermute x3, waiting for transfers between devices, shards(): lax.ppermute(picked, 'sub', [(i, (i + step) % sub) for i in range(sub)])  5.34 us
  transfers between devices with their start and end apart: 9, of which 6 were waited for; matrix products, arithmetic and copies ran while one was open for 0% of the time, Pallas kernels for 0%

profile of v2, /device:TPU:1, one launch (start us, length us, event | category | flops | bytes accessed | tf_op | source)
XLA Modules:
  0.0 255.7 jit_solution(16355757185955172241)
XLA Ops:
  7.2 0.0 copy-start.1
  7.2 0.0 copy-start.2
  7.2 1.6 copy.9
  8.8 0.7 convert_element_type.3
  9.4 0.1 broadcast_multiply_fusion
  9.5 30.6 %all_to_all.15 = f32[128,16,128]{2,1,0:T(8,128)S(1)} all-to-all(f32[128,16,128]{2,1,0:T(8,128)S(1)} %bitcast.15), channel_id=1, replica_groups=mesh['fly'=16,'sub'=8] {'fly','sub'}, dimensions={0} | all-to-all | bytes 2097152 | tf_op jit(solution)/shard_map/all_to_all | solution.py:339
  40.2 0.0 copy-start
  40.2 0.8 copy-done
  40.9 2.0 across_devices.1
  42.9 4.3 %all-to-all-start.1 = ((f32[128,16,128]{2,1,0:T(8,128)}), f32[128,16,128]{2,1,0:T(8,128)S(1)}, u32[]{:S(2)}, u32[]{:S(2)}) async-start(f32[128,16,128]{2,1,0:T(8,128)} %bitcast.5), calls=%async_computation.1 | async-start | bytes 2097152 | tf_op jit(solution)/shard_map/all_to_all | solution.py:342
  47.3 0.0 all-gather.3.cloned.1.call-start
  47.3 0.0 copy-done.2
  47.4 0.0 copy-done.1
  47.4 0.6 gather_fusion
  48.0 18.8 %all-to-all-done.1 = f32[128,16,128]{2,1,0:T(8,128)S(1)} async-done(((f32[128,16,128]{2,1,0:T(8,128)}), f32[128,16,128]{2,1,0:T(8,128)S(1)}, u32[]{:S(2)}, u32[]{:S(2)}) %all-to-all-start.1) | async-done | bytes 1048608 | tf_op jit(solution)/shard_map/all_to_all | solution.py:342
  66.7 1.2 fusion.refs_0_
  67.9 0.1 collective-permute-start
  68.0 1.4 collective-permute-start.1
  69.4 1.3 collective-permute-start.2
  70.7 1.6 collective-permute-start.3
  72.3 5.3 %collective-permute-done.refs_1_ = f32[32,2048]{1,0:T(8,128)S(1)} collective-permute-done((f32[32,2048]{1,0:T(8,128)S(1)}, f32[32,2048]{1,0:T(8,128)S(1)}, u32[]{:S(2)}, u32[]{:S(2)}) %collective-permute-start) | collective-permute-done | bytes 262176 | tf_op jit(solution)/shard_map/ppermute | solution.py:353
  77.6 5.9 %collective-permute-start.4 = (f32[32,2048]{1,0:T(8,128)S(1)}, f32[32,2048]{1,0:T(8,128)S(1)}, u32[]{:S(2)}, u32[]{:S(2)}) collective-permute-start(f32[32,2048]{1,0:T(8,128)S(1)} %collective-permute-done.refs_1_), channel_id=1, source_target_pairs={{0,1},{1,0},{2,3},{3,2},{4,5},{5,4},{6,7},{7,6},{8,9},{9,8},{10,11... | collective-permute-start | bytes 786440 | tf_op jit(solution)/shard_map/ppermute | solution.py:354
  83.5 0.0 collective-permute-done.1.refs_2_
  83.5 0.0 collective-permute-start.5
  83.5 0.0 collective-permute-done.2.refs_3_
  83.5 0.6 collective-permute-start.6
  84.2 0.0 collective-permute-done.3.refs_4_
  84.2 0.5 collective-permute-done.4.refs_5_
  84.7 0.4 collective-permute-done.5.refs_6_
  85.1 0.4 collective-permute-done.6.refs_7_
  85.5 1.9 gram_share.1
  87.4 19.7 %all_to_all.16 = f32[16,136,128]{2,1,0:T(8,128)S(1)} all-to-all(f32[16,136,128]{2,1,0:T(8,128)S(1)} %bitcast.11), channel_id=1, replica_groups=mesh['fly'=16,'sub'=8] {'fly'}, dimensions={0} | all-to-all | bytes 2228224 | tf_op jit(solution)/shard_map/all_to_all | solution.py:357
  107.1 0.1 reduce_sum.9
  107.2 0.6 pad_maximum_fusion
  107.8 0.0 all-gather.3.cloned.1.call-update
  108.5 68.9 %all-gather.3.cloned.1.call-done = f32[18432,128]{1,0:T(8,128)} async-done(((f32[144,128]{1,0:T(8,128)}), f32[18432,128]{1,0:T(8,128)}) %all-gather.3.cloned.1.call-update) | async-done | bytes 9437200 | tf_op jit(solution)/shard_map/all_gather | solution.py:359
  177.4 1.2 slice_reduce_fusion
  178.6 0.7 reshape_squeeze.3
  179.3 69.6 %cholesky.1 = f32[16,2048]{1,0:T(8,128)} custom-call(s32[1]{0:T(128)} %bitcast.place_ref, f32[1]{0:T(128)S(6)} %copy.10.ridge_ref, f32[128,144,128]{2,1,0:T(8,128)} %bitcast.14), custom_call_target="tpu_custom_call" | custom-call | tf_op jit(solution)/shard_map/cholesky/pallas_call | solution.py:249
  (4 shorter events, 0.0 us)
Async XLA Ops:
  7.2 40.2 %copy-start.1 = (f32[128,128]{1,0:T(8,128)S(1)}, f32[128,128]{1,0:T(8,128)}, u32[]{:S(2)}) copy-start(f32[128,128]{1,0:T(8,128)} %constant.37.clone) | copy-start | bytes 196612
  7.2 40.2 %copy-start.2 = (s32[32]{0:T(128)S(1)}, s32[32]{0:T(128)}, u32[]{:S(2)}) copy-start(s32[32]{0:T(128)} %param.8) | copy-start | bytes 388
  40.2 0.8 copy-start
  42.9 23.8 %all-to-all-start.1 = ((f32[128,16,128]{2,1,0:T(8,128)}), f32[128,16,128]{2,1,0:T(8,128)S(1)}, u32[]{:S(2)}, u32[]{:S(2)}) async-start(f32[128,16,128]{2,1,0:T(8,128)} %bitcast.5), calls=%async_computation.1 | async-start | bytes 2097152 | tf_op jit(solution)/shard_map/all_to_all | solution.py:342
  47.3 130.1 %all-gather.3.cloned.1.call-start = ((), (), s32[]{:S(2)}) async-start(), calls=%async_computation.3 | async-start | bytes 9510912 | tf_op jit(solution)/shard_map/all_gather | solution.py:359
  67.9 9.7 %collective-permute-start = (f32[32,2048]{1,0:T(8,128)S(1)}, f32[32,2048]{1,0:T(8,128)S(1)}, u32[]{:S(2)}, u32[]{:S(2)}) collective-permute-start(f32[32,2048]{1,0:T(8,128)S(1)} %fusion.refs_0_), channel_id=1, source_target_pairs={{0,2},{1,3},{2,4},{3,5},{4,6},{5,7},{6,0},{7,1},{8,10},{9,11},{10,... | collective-permute-start | bytes 786440 | tf_op jit(solution)/shard_map/ppermute | solution.py:353
  68.0 15.5 %collective-permute-start.1 = (f32[32,2048]{1,0:T(8,128)S(1)}, f32[32,2048]{1,0:T(8,128)S(1)}, u32[]{:S(2)}, u32[]{:S(2)}) collective-permute-start(f32[32,2048]{1,0:T(8,128)S(1)} %fusion.refs_0_), channel_id=1, source_target_pairs={{0,4},{1,5},{2,6},{3,7},{4,0},{5,1},{6,2},{7,3},{8,12},{9,13},{10,... | collective-permute-start | bytes 786440 | tf_op jit(solution)/shard_map/ppermute | solution.py:353
  69.4 14.2 %collective-permute-start.2 = (f32[32,2048]{1,0:T(8,128)S(1)}, f32[32,2048]{1,0:T(8,128)S(1)}, u32[]{:S(2)}, u32[]{:S(2)}) collective-permute-start(f32[32,2048]{1,0:T(8,128)S(1)} %fusion.refs_0_), channel_id=1, source_target_pairs={{0,6},{1,7},{2,0},{3,1},{4,2},{5,3},{6,4},{7,5},{8,14},{9,15},{10,... | collective-permute-start | bytes 786440 | tf_op jit(solution)/shard_map/ppermute | solution.py:353
  70.7 13.5 %collective-permute-start.3 = (f32[32,2048]{1,0:T(8,128)S(1)}, f32[32,2048]{1,0:T(8,128)S(1)}, u32[]{:S(2)}, u32[]{:S(2)}) collective-permute-start(f32[32,2048]{1,0:T(8,128)S(1)} %fusion.refs_0_), channel_id=1, source_target_pairs={{0,1},{1,0},{2,3},{3,2},{4,5},{5,4},{6,7},{7,6},{8,9},{9,8},{10,11... | collective-permute-start | bytes 786440 | tf_op jit(solution)/shard_map/ppermute | solution.py:354
  77.6 7.1 %collective-permute-start.4 = (f32[32,2048]{1,0:T(8,128)S(1)}, f32[32,2048]{1,0:T(8,128)S(1)}, u32[]{:S(2)}, u32[]{:S(2)}) collective-permute-start(f32[32,2048]{1,0:T(8,128)S(1)} %collective-permute-done.refs_1_), channel_id=1, source_target_pairs={{0,1},{1,0},{2,3},{3,2},{4,5},{5,4},{6,7},{7,6},{8,9},{9,8},{10,11... | collective-permute-start | bytes 786440 | tf_op jit(solution)/shard_map/ppermute | solution.py:354
  83.5 1.5 collective-permute-start.5
  83.5 1.9 collective-permute-start.6
Sparse Core Ops, SparseCore 0:
  108.0 69.3 all-gather.2
